TPU v7x, 256 devices: a whole 4x4x8 slice. The times are simulated.
256 devices in a mesh: expert: 8 (over y, x_lo), dp: 32 (over x_hi, z, core).
Axes of the slice: x: 4 (x_hi: 2, x_lo: 2; x = x_hi * 2 + x_lo), y: 4, z: 8, core: 2. Of those that a mesh axis runs over, the one named last changes fastest.
Arguments:
- tokens: bfloat16 [4096, 3072], P(('expert', 'dp')), may hold values from -6 to 6
- cotangent: bfloat16 [4096, 3072], P(('expert', 'dp')), may hold values from -6 to 6
- experts: int32 [4096, 2], P(('expert', 'dp')), may hold values from 0 to 7, all different within a row; in each aligned block of 16 rows (0 to 15, 16 to 31, ...) at most 8 rows name the same one
- gate_weights: float32 [4096, 2], P(('expert', 'dp')), may hold values from 0.1 to 1
- w_up: bfloat16 [8, 3072, 8192], P('expert', None, 'dp'), may hold values from -0.109375 to 0.109375
- master: float32 [8, 8192, 3072], P(None, 'dp', 'expert'), may hold values from -6 to 6
- moment_one: bfloat16 [8, 8192, 3072], P(None, 'dp', 'expert'), may hold values from -18 to 18
- moment_two: bfloat16 [8, 8192, 3072], P(None, 'dp', 'expert'), may hold values from 10 to 100
Outputs:
- new_master: float32 [8, 8192, 3072], P('expert', 'dp')
Inputs may be any that keep to these rules, and one draw needn't show every extreme that they name: Each token names two different experts; the tokens of one device name any expert at most 8 times, a bound that some block reaches.
All inputs are finite; a program needn't handle non-finite values.
Results may differ from a plain program's by a relative error of at most 0.0003.
Values may be sent and summed in bfloat16 or wider, within the bound.
A program may use at most 128 MiB of HBM per device.

v0:
```python
import jax
import jax.numpy as jnp
from jax import lax
from jax.sharding import PartitionSpec as P

CAP = 8


beta_one = 0.9
beta_two = 0.95
corr_one = 1.0 - (0.9**50) ** 2
corr_two = 1.0 - (0.95**50) ** 2
learn_rate = 0.2
weight_decay = 0.1
epsilon = 1e-08


def adam_update(master, moment_one, moment_two, gradient):
    first = beta_one * moment_one.astype(jnp.float32) + (1.0 - beta_one) * gradient
    second = beta_two * moment_two.astype(jnp.float32) + (1.0 - beta_two) * gradient * gradient
    update = first / corr_one / (jnp.sqrt(second / corr_two) + epsilon)
    return master - learn_rate * (update + weight_decay * master)


def body(tokens, cotangent, experts, gate_weights, w_up, master, moment_one, moment_two):
    count_experts = master.shape[0]
    model_width = tokens.shape[1]
    choices_each = experts.shape[1]
    flat_ids = experts.reshape(-1)
    onehot = (flat_ids[:, None] == jnp.arange(count_experts, dtype=jnp.int32)[None, :]).astype(
        jnp.int32
    )
    position = jnp.sum((jnp.cumsum(onehot, axis=0) - 1) * onehot, axis=1)
    target = flat_ids * CAP + position
    placing = (jnp.arange(count_experts * CAP, dtype=jnp.int32)[:, None] == target[None, :]).astype(
        jnp.bfloat16
    )
    token_copies = jnp.repeat(tokens, choices_each, axis=0)
    scaled = (
        jnp.repeat(cotangent.astype(jnp.float32), choices_each, axis=0)
        * gate_weights.reshape(-1)[:, None]
    ).astype(jnp.bfloat16)
    send_tokens = jnp.dot(placing, token_copies, preferred_element_type=jnp.float32).astype(
        jnp.bfloat16
    )
    send_scaled = jnp.dot(placing, scaled, preferred_element_type=jnp.float32).astype(jnp.bfloat16)
    send_tokens = send_tokens.reshape(count_experts, CAP, model_width)
    send_scaled = send_scaled.reshape(count_experts, CAP, model_width)
    got_tokens, got_scaled = (
        lax.all_to_all(send_tokens, "expert", split_axis=0, concat_axis=0, tiled=True),
        lax.all_to_all(send_scaled, "expert", split_axis=0, concat_axis=0, tiled=True),
    )
    got_tokens = got_tokens.reshape(-1, model_width)
    got_scaled = got_scaled.reshape(-1, model_width)
    local_up = w_up[0]
    piece_tokens = lax.all_gather(got_tokens, "dp", axis=0, tiled=True)
    piece_scaled = lax.all_gather(got_scaled, "dp", axis=0, tiled=True)
    hidden = jax.nn.silu(
        jnp.dot(piece_tokens, local_up, preferred_element_type=jnp.float32)
    ).astype(jnp.bfloat16)
    gradient = lax.dot_general(
        hidden, piece_scaled, (((0,), (0,)), ((), ())), preferred_element_type=jnp.float32
    )
    gradient = gradient[None]
    spread = lax.all_to_all(
        gradient.astype(jnp.bfloat16), "expert", split_axis=2, concat_axis=0, tiled=True
    ).astype(gradient.dtype)
    fresh_master = adam_update(master, moment_one, moment_two, spread)
    return lax.all_to_all(fresh_master, "expert", split_axis=0, concat_axis=2, tiled=True)


def solution(mesh):
    placed = (
        P(("expert", "dp"), None),
        P(("expert", "dp"), None),
        P(("expert", "dp"), None),
        P(("expert", "dp"), None),
        P("expert", None, "dp"),
        P(None, "dp", "expert"),
        P(None, "dp", "expert"),
        P(None, "dp", "expert"),
    )
    return jax.shard_map(
        body, mesh=mesh, in_specs=placed, out_specs=P("expert", "dp", None), check_vma=False
    )
```

profile of v0, /device:TPU:1, one launch (start us, length us, event | category | flops | bytes accessed | tf_op | source)
XLA Modules:
  0.0 399.0 jit_solution(3929386972154533601)
XLA Ops:
  6.5 0.9 copy.17
  7.4 0.1 reshape.36
  7.5 0.1 fusion.21
  7.6 0.1 reduce_window_sum.11
  7.7 0.2 select_reduce_fusion
  7.8 1.0 broadcast_in_dim.5
  8.9 0.3 reshape.40
  9.1 0.8 copy.18
  9.9 0.1 mul.66
  10.0 0.3 fusion.2
  10.3 13.6 %all_to_all.37 = bf16[8,8,3072]{2,1,0:T(8,128)(2,1)} all-to-all(bf16[8,8,3072]{2,1,0:T(8,128)(2,1)S(1)} %fusion.2), channel_id=1, replica_groups=mesh['expert'=8,'dp'=32] {'expert'}, dimensions={0} | all-to-all | bytes 786432 | tf_op jit(solution)/shard_map/all_to_all | solution.py:51
  23.9 0.0 all-gather.5.cloned.1.call-update
  23.9 0.0 all-gather.3.cloned.1.call-start
  24.0 0.1 broadcast_in_dim.4
  24.1 0.1 reshape.37
  24.2 0.2 fusion.1
  24.4 10.1 %all_to_all.38 = bf16[8,8,3072]{2,1,0:T(8,128)(2,1)} all-to-all(bf16[8,8,3072]{2,1,0:T(8,128)(2,1)S(1)} %fusion.1), channel_id=1, replica_groups=mesh['expert'=8,'dp'=32] {'expert'}, dimensions={0} | all-to-all | bytes 786432 | tf_op jit(solution)/shard_map/all_to_all | solution.py:50
  34.6 0.0 all-gather.3.cloned.1.call-update
  34.6 109.2 %all-gather.5.cloned.1.call-done = bf16[2048,3072]{1,0:T(8,128)(2,1)} async-done(((bf16[64,3072]{1,0:T(8,128)(2,1)}), bf16[2048,3072]{1,0:T(8,128)(2,1)}) %all-gather.5.cloned.1.call-update) | async-done | bytes 12582928 | tf_op jit(solution)/shard_map/all_gather | solution.py:57
  143.8 117.0 %all-gather.3.cloned.1.call-done = bf16[2048,3072]{1,0:T(8,128)(2,1)} async-done(((bf16[64,3072]{1,0:T(8,128)(2,1)}), bf16[2048,3072]{1,0:T(8,128)(2,1)}) %all-gather.3.cloned.1.call-update) | async-done | bytes 12582928 | tf_op jit(solution)/shard_map/all_gather | solution.py:56
  260.8 0.0 copy-done
  260.8 21.1 %fusion = bf16[1,256,3072]{2,1,0:T(8,128)(2,1)S(1)} fusion(bf16[2048,3072]{1,0:T(8,128)(2,1)} %all-gather.5.cloned.1.call-done, bf16[2048,3072]{1,0:T(8,128)(2,1)} %all-gather.3.cloned.1.call-done, bf16[1,3072,256]{2,1,0:T(8,128)(2,1)S(1)} %copy-done), kind=kOutput, calls=%fused_computation.2 | convolution fusion | flops 6445858816 | bytes 28311552 | tf_op jit(solution)/shard_map/dot_general | solution.py:61
  281.9 5.2 %copy.19 = bf16[1,256,3072]{1,0,2:T(2,128)(2,1)} copy(bf16[1,256,3072]{2,1,0:T(8,128)(2,1)S(1)} %fusion) | data formatting | bytes 3145728 | tf_op jit(solution)/shard_map/convert_element_type | solution.py:66
  287.1 0.5 broadcast.23
  287.6 16.7 %reduce = bf16[3072,256]{1,0:T(8,128)(2,1)S(1)} reduce(bf16[3072,1,256]{2,1,0:T(2,128)(2,1)} %bitcast.40, bf16[]{:T(256)} %broadcast.23), dimensions={1}, to_apply=%bitcast.35.reduce_sub_computation | reduce | bytes 3145730
  304.3 1.8 reshape.45
  306.1 24.6 %all_to_all.39 = bf16[8,2,49152]{2,1,0:T(2,128)(2,1)S(1)} all-to-all(bf16[8,2,49152]{2,1,0:T(2,128)(2,1)} %reshape.45), channel_id=1, replica_groups=mesh['expert'=8,'dp'=32] {'expert'}, dimensions={0} | all-to-all | bytes 3145728 | tf_op jit(solution)/shard_map/all_to_all | solution.py:65
  330.7 3.9 reshape.46
  334.6 8.8 %copy.20 = f32[1,256,8,384]{3,1,2,0:T(8,128)} copy(bf16[1,256,8,384]{1,0,3,2:T(2,128)(2,1)} %bitcast.41) | data formatting | bytes 4718592 | tf_op jit(solution)/shard_map/convert_element_type | solution.py:67
  343.4 5.8 %multiply_subtract_fusion = f32[8,256,384]{2,1,0:T(8,128)S(1)} fusion(f32[8,256,384]{2,1,0:T(8,128)} %param.13, f32[1,256,8,384]{3,1,2,0:T(8,128)} %copy.20, bf16[8,256,384]{2,1,0:T(8,128)(2,1)S(1)} %copy-done.1, bf16[8,256,384]{2,1,0:T(8,128)(2,1)} %param.14), kind=kLoop, calls=%fused_computation.16 | loop fusion | flops 13369344 | bytes 12582912 | tf_op jit(solution)/shard_map/sub | solution.py:22
  349.2 40.9 %all_to_all.40 = f32[8,256,384]{2,1,0:T(8,128)S(1)} all-to-all(f32[8,256,384]{2,1,0:T(8,128)S(1)} %multiply_subtract_fusion), channel_id=1, replica_groups=mesh['expert'=8,'dp'=32] {'expert'}, dimensions={0} | all-to-all | bytes 6291456 | tf_op jit(solution)/shard_map/all_to_all | solution.py:69
  390.1 2.1 copy.22
  (7 shorter events, 0.0 us)
Async XLA Ops:
  6.5 254.3 %copy-start = (bf16[1,3072,256]{2,1,0:T(8,128)(2,1)S(1)}, bf16[1,3072,256]{2,1,0:T(8,128)(2,1)}, u32[]{:S(2)}) copy-start(bf16[1,3072,256]{2,1,0:T(8,128)(2,1)} %param.12) | copy-start | bytes 4718596
  6.5 17.5 %copy-start.2 = (bf16[16,3072]{1,0:T(8,128)(2,1)S(1)}, bf16[16,3072]{1,0:T(8,128)(2,1)}, u32[]{:S(2)}) copy-start(bf16[16,3072]{1,0:T(8,128)(2,1)} %param.8) | copy-start | bytes 294916
  6.5 137.2 %all-gather.5.cloned.1.call-start = ((), (), s32[]{:S(2)}) async-start(), calls=%async_computation.5 | async-start | bytes 12976128 | tf_op jit(solution)/shard_map/all_gather | solution.py:57
  23.9 236.9 %all-gather.3.cloned.1.call-start = ((), (), s32[]{:S(2)}) async-start(), calls=%async_computation.4 | async-start | bytes 12976128 | tf_op jit(solution)/shard_map/all_gather | solution.py:56
  334.6 8.8 %copy-start.1 = (bf16[8,256,384]{2,1,0:T(8,128)(2,1)S(1)}, bf16[8,256,384]{2,1,0:T(8,128)(2,1)}, u32[]{:S(2)}) copy-start(bf16[8,256,384]{2,1,0:T(8,128)(2,1)} %param.15) | copy-start | bytes 4718596
Sparse Core Ops, SparseCore 0:
  24.1 119.6 all-gather.4
  146.5 114.2 all-gather.2
where the time goes:
time: 400 us; the launch traced here: 399 us
  waiting for transfers between devices  226 us (56%)
  blocking collectives  89.2 us (22%)
  local copies, waits for them, and re-layouts  25.5 us (6%)
  other arithmetic  22.8 us (6%)
  matrix products  21.7 us (5%)
  between operations  13.5 us (3%)
    all_gather x1, waiting for transfers between devices, body(): piece_tokens = lax.all_gather(got_tokens, 'dp', axis=0, tiled=True)  117 us
    all_gather x1, waiting for transfers between devices, body(): piece_scaled = lax.all_gather(got_scaled, 'dp', axis=0, tiled=True)  109 us
    all_to_all x1, blocking collectives, body(): lax.all_to_all(fresh_master, 'expert', split_axis=0, concat_axis=2, tiled...  40.9 us
    all_to_all x1, blocking collectives, body(): lax.all_to_all(gradient.astype(jnp.bfloat16), 'expert', split_axis=2, con...  24.6 us
    dot_general x1, matrix products, body(): lax.dot_general(hidden, piece_scaled, (((0,), (0,)), ((), ())), preferred...  21.1 us
    unnamed x1, other arithmetic  16.7 us
    all_to_all x1, blocking collectives, body(): lax.all_to_all(send_scaled, 'expert', split_axis=0, concat_axis=0, tiled=...  13.6 us
    all_to_all x1, blocking collectives, body(): lax.all_to_all(send_tokens, 'expert', split_axis=0, concat_axis=0, tiled=...  10.1 us
  transfers between devices with their start and end apart: 2, of which 2 were waited for; matrix products, arithmetic and copies ran while one was open for 0% of the time, Pallas kernels for 0%

commit v1 on v0

v1 whole, which is shorter than its diff:
```python
import functools

import jax
import jax.numpy as jnp
from jax import lax
from jax.experimental import pallas as pl
from jax.experimental.pallas import tpu as pltpu
from jax.sharding import PartitionSpec as P

CAP = 8
MESH = pl.DeviceIdType.MESH
FACES = 2
CORES = 2
PIECE = 2 * CAP
COLS = 512

beta_one = 0.9
beta_two = 0.95
corr_one = 1.0 - (0.9**50) ** 2
corr_two = 1.0 - (0.95**50) ** 2
learn_rate = 0.2
weight_decay = 0.1
epsilon = 1e-08


def adam_update(master, moment_one, moment_two, gradient):
    first = beta_one * moment_one.astype(jnp.float32) + (1.0 - beta_one) * gradient
    second = beta_two * moment_two.astype(jnp.float32) + (1.0 - beta_two) * gradient * gradient
    update = first / corr_one / (jnp.sqrt(second / corr_two) + epsilon)
    return master - learn_rate * (update + weight_decay * master)


def kernel(
    E,
    Z,
    experts_ref,
    gates_ref,
    tokens_ref,
    cotangent_ref,
    up_ref,
    master_ref,
    one_ref,
    two_ref,
    grad_ref,
    out_master,
    out_one,
    out_two,
    send,
    buf,
    wbuf,
    acts,
    acc,
    give,
    take,
    disp_s,
    disp_r,
    ring_s,
    ring_r,
    state_s,
    state_r,
    up_s,
    up_r,
    tail_s,
    tail_r,
    local_sem,
):
    e = lax.axis_index("expert")
    d = lax.axis_index("dp")
    c = lax.rem(d, CORES)
    z = lax.rem(lax.div(d, CORES), Z)
    xh = lax.div(d, CORES * Z)
    unit = E * PIECE
    half = Z // 2
    D = tokens_ref.shape[1]
    F = up_ref.shape[1]
    width = D // E

    def dp_of(face, layer, core):
        return (face * Z + layer) * CORES + core

    other_face = dp_of(1 - xh, z, c)
    sibling = dp_of(xh, z, 1 - c)
    ahead = dp_of(xh, lax.rem(z + 1, Z), c)
    behind = dp_of(xh, lax.rem(z + Z - 1, Z), c)

    def peer(k):
        return lax.rem(e + k, E)

    barrier = pltpu.get_barrier_semaphore()
    greet = [(peer(k), d) for k in range(1, E)] + [(peer(k), other_face) for k in range(E)]
    greet += [(e, ahead), (e, behind), (e, sibling)]
    for who in greet:
        pl.semaphore_signal(barrier, inc=1, device_id=who, device_id_type=MESH)

    own_up = pltpu.make_async_copy(up_ref, wbuf.at[c], local_sem.at[0])
    own_up.start()

    T = tokens_ref.shape[0]
    row = lax.broadcasted_iota(jnp.int32, (unit, T), 0)
    expert_of = lax.div(row, PIECE)
    slot = lax.rem(row, PIECE)
    is_scaled = slot >= CAP
    slot = lax.rem(slot, CAP)
    first_choice = experts_ref[0:1, :] == expert_of
    second_choice = experts_ref[1:2, :] == expert_of
    named = jnp.logical_or(first_choice, second_choice)
    earlier = lax.broadcasted_iota(jnp.int32, (T, T), 0) < lax.broadcasted_iota(jnp.int32, (T, T), 1)
    place = jnp.dot(
        jnp.where(named, 1.0, 0.0).astype(jnp.bfloat16),
        jnp.where(earlier, 1.0, 0.0).astype(jnp.bfloat16),
        preferred_element_type=jnp.float32,
    )
    hit = jnp.logical_and(named, place == slot.astype(jnp.float32))
    pick_token = jnp.where(jnp.logical_and(hit, jnp.logical_not(is_scaled)), 1.0, 0.0).astype(jnp.bfloat16)
    scaled_hit = jnp.where(jnp.logical_and(hit, is_scaled), 1.0, 0.0)
    pick_scaled = scaled_hit.astype(jnp.bfloat16)
    gate = jnp.where(first_choice, gates_ref[0:1, :], 0.0) + jnp.where(second_choice, gates_ref[1:2, :], 0.0)
    gate = jnp.sum(gate * scaled_hit, axis=1, keepdims=True)

    @pl.loop(0, D // COLS)
    def _(j):
        cols = pl.ds(pl.multiple_of(j * COLS, COLS), COLS)
        rows_token = jnp.dot(pick_token, tokens_ref[:, cols], preferred_element_type=jnp.float32)
        rows_scaled = jnp.dot(pick_scaled, cotangent_ref[:, cols], preferred_element_type=jnp.float32)
        send[:, cols] = (rows_token + rows_scaled * gate).astype(jnp.bfloat16)

    pl.semaphore_wait(barrier, len(greet))

    def piece_of(k):
        return send.at[pl.ds(pl.multiple_of(peer(k) * PIECE, PIECE), PIECE)]

    def landing(stream):
        return buf.at[0, pl.ds(pl.multiple_of(stream * unit + e * PIECE, PIECE), PIECE)]

    dispatch = {}
    for stream, where in ((0, d), (1, other_face)):
        for k in range(E):
            if stream == 0 and k == 0:
                continue
            dispatch[stream, k] = pltpu.make_async_remote_copy(
                src_ref=piece_of(k),
                dst_ref=landing(stream),
                send_sem=disp_s.at[stream, k],
                recv_sem=disp_r.at[stream, k],
                device_id=(peer(k), where),
                device_id_type=MESH,
            )
            dispatch[stream, k].start()
    own_piece = pltpu.make_async_copy(piece_of(0), landing(0), local_sem.at[1])
    own_piece.start()
    give_up = pltpu.make_async_remote_copy(
        src_ref=up_ref,
        dst_ref=wbuf.at[c],
        send_sem=up_s,
        recv_sem=up_r,
        device_id=(e, sibling),
        device_id_type=MESH,
    )
    give_up.start()

    def hops(stream, way):
        return half - (stream ^ way)

    def where_is(stream, way, s):
        if s == 0:
            return buf.at[0, pl.ds(stream * unit, unit)]
        if s == half:
            return buf.at[2 * half - 1, pl.ds(stream * unit, unit)]
        return buf.at[2 * s - 1 + stream, pl.ds(way * unit, unit)]

    ring = {}
    for stream in range(2):
        for way, neighbour in ((0, ahead), (1, behind)):
            for s in range(hops(stream, way)):
                ring[stream, way, s] = pltpu.make_async_remote_copy(
                    src_ref=where_is(stream, way, s),
                    dst_ref=where_is(stream, way, s + 1),
                    send_sem=ring_s.at[stream, way, s],
                    recv_sem=ring_r.at[stream, way, s],
                    device_id=(e, neighbour),
                    device_id_type=MESH,
                )

    def forward(stream, way, s):
        if (stream, way, s) in ring:
            ring[stream, way, s].start()

    for stream in range(2):
        for k in range(E):
            if (stream, k) in dispatch:
                dispatch[stream, k].wait_recv()
        if stream == 0:
            own_piece.wait()
        for way in range(2):
            forward(stream, way, 0)

    own_cols = pl.ds(pl.multiple_of(e * width, width), width)
    state, own_state = [], []
    for k in range(1, E):
        for i, (src, dst) in enumerate(((master_ref, out_master), (one_ref, out_one), (two_ref, out_two))):
            state.append(
                pltpu.make_async_remote_copy(
                    src_ref=src.at[peer(k)],
                    dst_ref=dst.at[:, own_cols],
                    send_sem=state_s.at[i, k],
                    recv_sem=state_r.at[i, k],
                    device_id=(peer(k), d),
                    device_id_type=MESH,
                )
            )
            state[-1].start()
    for i, (src, dst) in enumerate(((master_ref, out_master), (one_ref, out_one), (two_ref, out_two))):
        own_state.append(pltpu.make_async_copy(src.at[e], dst.at[:, own_cols], local_sem.at[2 + i]))
        own_state[-1].start()

    own_up.wait()
    give_up.wait_recv()

    batch_rows = 2 * unit

    def hidden(b):
        @pl.loop(0, CORES)
        def _(h):
            up = jnp.dot(buf[b], wbuf[h], preferred_element_type=jnp.float32)
            up = up / (1.0 + jnp.exp(-up))
            up = up.reshape(batch_rows // PIECE, PIECE, F)[:, :CAP]
            up = jnp.concatenate([jnp.zeros_like(up), up], axis=1).reshape(batch_rows, F)
            acts[pl.ds(pl.multiple_of(h * F, F), F), :] = up.T.astype(jnp.bfloat16)

    def product(b, cols):
        return jnp.dot(acts[...], buf[b, :, cols], preferred_element_type=jnp.float32)

    def compute(b):
        hidden(b)

        @pl.loop(0, D // COLS)
        def _(j):
            cols = pl.ds(pl.multiple_of(j * COLS, COLS), COLS)
            if b == 0:
                acc[:, cols] = product(b, cols)
            else:
                acc[:, cols] += product(b, cols)

    compute(0)
    for s in range(1, half):
        for stream in range(2):
            for way in range(2):
                ring[stream, way, s - 1].wait_recv()
                forward(stream, way, s)
            compute(2 * s - 1 + stream)
    last = 2 * half - 1
    ring[0, 0, half - 1].wait_recv()
    ring[1, 1, half - 1].wait_recv()
    hidden(last)

    theirs = pl.ds(pl.multiple_of((1 - c) * F, F), F)
    mine = pl.ds(pl.multiple_of(c * F, F), F)
    tail = []
    for j in range(D // COLS):
        cols = pl.ds(j * COLS, COLS)
        acc[:, cols] += product(last, cols)
        give[j] = acc[theirs, cols].astype(jnp.bfloat16)
        tail.append(
            pltpu.make_async_remote_copy(
                src_ref=give.at[j],
                dst_ref=take.at[j],
                send_sem=tail_s.at[j],
                recv_sem=tail_r.at[j],
                device_id=(e, sibling),
                device_id_type=MESH,
            )
        )
        tail[-1].start()
    for j in range(D // COLS):
        cols = pl.ds(j * COLS, COLS)
        tail[j].wait_recv()
        grad_ref[:, cols] = acc[mine, cols] + take[j].astype(jnp.float32)

    for copy in state:
        copy.wait()
    for copy in own_state:
        copy.wait()
    for copy in list(dispatch.values()) + [give_up] + list(ring.values()) + tail:
        copy.wait_send()


def body(E, Z, tokens, cotangent, experts, gate_weights, w_up, master, moment_one, moment_two):
    D = tokens.shape[1]
    F = w_up.shape[2]
    unit = E * PIECE
    half = Z // 2
    in_vmem = pl.BlockSpec(memory_space=pltpu.VMEM)
    anywhere = pl.BlockSpec(memory_space=pl.ANY)
    grad, far_master, far_one, far_two = pl.pallas_call(
        functools.partial(kernel, E, Z),
        out_shape=(
            jax.ShapeDtypeStruct((F, D), jnp.float32),
            jax.ShapeDtypeStruct((F, D), jnp.float32),
            jax.ShapeDtypeStruct((F, D), jnp.bfloat16),
            jax.ShapeDtypeStruct((F, D), jnp.bfloat16),
        ),
        in_specs=[in_vmem] * 4 + [anywhere] * 4,
        out_specs=(in_vmem, anywhere, anywhere, anywhere),
        scratch_shapes=[
            pltpu.VMEM((unit, D), jnp.bfloat16),
            pltpu.VMEM((Z, 2 * unit, D), jnp.bfloat16),
            pltpu.VMEM((CORES, D, F), jnp.bfloat16),
            pltpu.VMEM((CORES * F, 2 * unit), jnp.bfloat16),
            pltpu.VMEM((CORES * F, D), jnp.float32),
            pltpu.VMEM((D // COLS, F, COLS), jnp.bfloat16),
            pltpu.VMEM((D // COLS, F, COLS), jnp.bfloat16),
            pltpu.SemaphoreType.DMA((2, E)),
            pltpu.SemaphoreType.DMA((2, E)),
            pltpu.SemaphoreType.DMA((2, 2, half)),
            pltpu.SemaphoreType.DMA((2, 2, half)),
            pltpu.SemaphoreType.DMA((3, E)),
            pltpu.SemaphoreType.DMA((3, E)),
            pltpu.SemaphoreType.DMA,
            pltpu.SemaphoreType.DMA,
            pltpu.SemaphoreType.DMA((D // COLS,)),
            pltpu.SemaphoreType.DMA((D // COLS,)),
            pltpu.SemaphoreType.DMA((5,)),
        ],
        compiler_params=pltpu.CompilerParams(
            collective_id=0, has_side_effects=True, vmem_limit_bytes=48 * 1024 * 1024
        ),
    )(experts.T, gate_weights.T, tokens, cotangent, w_up[0], master, moment_one, moment_two)
    return adam_update(far_master, far_one, far_two, grad)[None]


def solution(mesh):
    E = mesh.shape["expert"]
    Z = mesh.shape["dp"] // (FACES * CORES)
    placed = (
        P(("expert", "dp"), None),
        P(("expert", "dp"), None),
        P(("expert", "dp"), None),
        P(("expert", "dp"), None),
        P("expert", None, "dp"),
        P(None, "dp", "expert"),
        P(None, "dp", "expert"),
        P(None, "dp", "expert"),
    )
    return jax.shard_map(
        functools.partial(body, E, Z),
        mesh=mesh,
        in_specs=placed,
        out_specs=P("expert", "dp", None),
        check_vma=False,
    )
```

time: 400 us -> 168 us (0.42)
  waiting for transfers between devices: 226 us -> 0 us
  Pallas kernels: 0 us -> 157 us
  blocking collectives: 89.2 us -> 0 us
  matrix products: 21.7 us -> 0 us
  local copies, waits for them, and re-layouts: 25.5 us -> 4.55 us
  other arithmetic: 22.8 us -> 5.64 us
  between operations: 13.5 us -> 0.01 us
    all_gather x2 -> x0, waiting for transfers between devices: 226 us -> none  [the longest x1 117 us: body(): piece_tokens = lax.all_gather(got_tokens, 'dp', axis=0, tiled=True)]
    pallas_call x0 -> x1, Pallas kernels: none -> 157 us  [body(): pl.pallas_call(functools.partial(kernel, E, Z), out_shape=(jax.ShapeDtype...]
    all_to_all x4 -> x0, blocking collectives: 89.2 us -> none  [the longest x1 40.9 us: body(): lax.all_to_all(fresh_master, 'expert', split_axis=0, concat_axis=2, tiled...]
    dot_general x3 -> x0, matrix products: 21.7 us -> none  [the longest x1 21.1 us: body(): lax.dot_general(hidden, piece_scaled, (((0,), (0,)), ((), ())), preferred...]
    unnamed x1 -> x0, other arithmetic: 16.7 us -> none
    convert_element_type x2 -> x0, local copies, waits for them, and re-layouts: 14 us -> none  [the longest x1 8.81 us: body(): spread = lax.all_to_all(gradient.astype(jnp.bfloat16), 'expert', split_ax...]
    sub x1 -> x0, other arithmetic: 5.81 us -> none  [adam_update(): return master - learn_rate * (update + weight_decay * master)]
    broadcast_in_dim x0 -> x1, other arithmetic: none -> 5.64 us  [body(): return adam_update(far_master, far_one, far_two, grad)[None]]
  transfers between devices with their start and end apart: 2 -> 0, of which waited for: 2 -> 0; matrix products, arithmetic and copies ran while one was open for 0% -> 0% of each run, Pallas kernels for 0% -> 0%
where the time goes in v1:
time: 168 us; the launch traced here: 167 us
  Pallas kernels  157 us (93%)
  other arithmetic  5.64 us (3%)
  local copies, waits for them, and re-layouts  4.55 us (3%)
    pallas_call x1, Pallas kernels, body(): pl.pallas_call(functools.partial(kernel, E, Z), out_shape=(jax.ShapeDtype...  157 us
    broadcast_in_dim x1, other arithmetic, body(): return adam_update(far_master, far_one, far_two, grad)[None]  5.64 us
    unnamed x10, local copies, waits for them, and re-layouts  4.55 us

profile of v1, /device:TPU:1, one launch (start us, length us, event | category | flops | bytes accessed | tf_op | source)
XLA Modules:
  0.0 167.4 jit_solution(12080072506514271156)
XLA Ops:
  0.0 0.0 copy-start
  0.0 1.4 copy-done
  1.4 0.0 copy-start.1
  1.4 0.9 copy-done.1
  2.3 0.0 copy-start.2
  2.3 0.9 copy-done.2
  3.2 0.0 copy-start.3
  3.2 0.7 copy-done.3
  3.9 0.0 copy-start.4
  3.9 0.7 copy-done.4
  4.6 157.2 %shard_map.82 = (f32[256,3072]{1,0:T(8,128)}, f32[256,3072]{1,0:T(8,128)}, bf16[256,3072]{1,0:T(8,128)(2,1)S(1)}, bf16[256,3072]{1,0:T(8,128)(2,1)S(1)}) custom-call(s32[2,16]{1,0:T(2,128)S(1)} %bitcast.6, f32[2,16]{1,0:T(2,128)S(1)} %bitcast.7, bf16[16,3072]{1,0:T(8,128)(2,1)S(1)} %copy-done.1, bf16[16,3072]{1,0:T(8,128)(2,1)S(1)} %copy-done.2, ...), custom_call_target="tpu_custom_call" | custom-call | tf_op jit(solution)/shard_map/pallas_call | solution.py:294
  161.7 5.6 %subtract_bitcast_fusion = f32[1,256,3072]{2,1,0:T(8,128)} fusion(f32[256,3072]{1,0:T(8,128)} %get-tuple-element.9, f32[256,3072]{1,0:T(8,128)} %get-tuple-element.11, bf16[256,3072]{1,0:T(8,128)(2,1)S(1)} %get-tuple-element.12, bf16[256,3072]{1,0:T(8,128)(2,1)S(1)} %get-tuple-element.10), kind=kLoop, calls=%fused_computation.7 | loop fusion | flops 13369344 | bytes 12582912 | tf_op jit(solution)/shard_map/broadcast_in_dim | solution.py:328
Async XLA Ops:
  0.0 1.4 copy-start
  1.4 0.9 copy-start.1
  2.3 0.9 copy-start.2
  3.2 0.7 copy-start.3
  3.9 0.7 copy-start.4

commit v2 on v1

v2 whole, which is shorter than its diff:
```python
import functools

import jax
import jax.numpy as jnp
from jax import lax
from jax.experimental import pallas as pl
from jax.experimental.pallas import tpu as pltpu
from jax.sharding import PartitionSpec as P

CAP = 8
MESH = pl.DeviceIdType.MESH
FACES = 2
CORES = 2
NEIGHBOURS = 2
PIECE = 2 * CAP
COLS = 512

beta_one = 0.9
beta_two = 0.95
corr_one = 1.0 - (0.9**50) ** 2
corr_two = 1.0 - (0.95**50) ** 2
learn_rate = 0.2
weight_decay = 0.1
epsilon = 1e-08


def adam_update(master, moment_one, moment_two, gradient):
    first = beta_one * moment_one.astype(jnp.float32) + (1.0 - beta_one) * gradient
    second = beta_two * moment_two.astype(jnp.float32) + (1.0 - beta_two) * gradient * gradient
    update = first / corr_one / (jnp.sqrt(second / corr_two) + epsilon)
    return master - learn_rate * (update + weight_decay * master)


def kernel(
    E,
    Z,
    experts_in,
    gates_in,
    tokens_in,
    cotangent_in,
    up_ref,
    master_ref,
    one_ref,
    two_ref,
    out_ref,
    experts_ref,
    gates_ref,
    tokens_ref,
    cotangent_ref,
    send,
    buf,
    wbuf,
    acts,
    acc,
    give,
    take,
    far_master,
    far_one,
    far_two,
    disp_s,
    disp_r,
    ring_s,
    ring_r,
    face_s,
    face_r,
    state_s,
    state_r,
    up_s,
    up_r,
    tail_s,
    tail_r,
    local_sem,
    out_sem,
):
    e = lax.axis_index("expert")
    d = lax.axis_index("dp")
    c = lax.rem(d, CORES)
    z = lax.rem(lax.div(d, CORES), Z)
    xh = lax.div(d, CORES * Z)
    unit = E * PIECE
    part = unit // 2
    half = Z // 2
    D = tokens_ref.shape[1]
    F = up_ref.shape[1]
    width = D // E
    steps = D // COLS

    def dp_of(face, layer, core):
        return (face * Z + layer) * CORES + core

    other_face = dp_of(1 - xh, z, c)
    sibling = dp_of(xh, z, 1 - c)
    ahead = dp_of(xh, lax.rem(z + 1, Z), c)
    behind = dp_of(xh, lax.rem(z + Z - 1, Z), c)

    Y = E // NEIGHBOURS
    offsets = [(0, 0), (0, 1), (1, 0), (Y - 1, 0)]
    offsets += [(dy, dx) for dy in range(Y) for dx in range(NEIGHBOURS) if (dy, dx) not in offsets]
    near = 4

    def peer(k):
        dy, dx = offsets[k]
        y = lax.rem(lax.div(e, NEIGHBOURS) + dy, Y)
        x = lax.rem(lax.rem(e, NEIGHBOURS) + dx, NEIGHBOURS)
        return y * NEIGHBOURS + x

    barrier = pltpu.get_barrier_semaphore()
    greet = [(peer(k), d) for k in range(1, E)] + [(peer(k), other_face) for k in range(E)]
    greet += [(e, ahead), (e, behind), (e, sibling)]
    for who in greet:
        pl.semaphore_signal(barrier, inc=1, device_id=who, device_id_type=MESH)

    loads = [
        pltpu.make_async_copy(src, dst, local_sem.at[5 + i])
        for i, (src, dst) in enumerate(
            (
                (experts_in, experts_ref),
                (gates_in, gates_ref),
                (tokens_in, tokens_ref),
                (cotangent_in, cotangent_ref),
            )
        )
    ]
    for copy in loads:
        copy.start()
    own_up = pltpu.make_async_copy(up_ref, wbuf.at[c], local_sem.at[0])
    own_up.start()
    for copy in loads:
        copy.wait()

    T = tokens_ref.shape[0]
    row = lax.broadcasted_iota(jnp.int32, (unit, T), 0)
    expert_of = lax.div(row, PIECE)
    slot = lax.rem(row, PIECE)
    is_scaled = slot >= CAP
    slot = lax.rem(slot, CAP)
    first_choice = experts_ref[0:1, :] == expert_of
    second_choice = experts_ref[1:2, :] == expert_of
    named = jnp.logical_or(first_choice, second_choice)
    earlier = lax.broadcasted_iota(jnp.int32, (T, T), 0) < lax.broadcasted_iota(jnp.int32, (T, T), 1)
    place = jnp.dot(
        jnp.where(named, 1.0, 0.0).astype(jnp.bfloat16),
        jnp.where(earlier, 1.0, 0.0).astype(jnp.bfloat16),
        preferred_element_type=jnp.float32,
    )
    hit = jnp.logical_and(named, place == slot.astype(jnp.float32))
    pick_token = jnp.where(jnp.logical_and(hit, jnp.logical_not(is_scaled)), 1.0, 0.0).astype(jnp.bfloat16)
    scaled_hit = jnp.where(jnp.logical_and(hit, is_scaled), 1.0, 0.0)
    pick_scaled = scaled_hit.astype(jnp.bfloat16)
    gate = jnp.where(first_choice, gates_ref[0:1, :], 0.0) + jnp.where(second_choice, gates_ref[1:2, :], 0.0)
    gate = jnp.sum(gate * scaled_hit, axis=1, keepdims=True)

    @pl.loop(0, steps)
    def _(j):
        cols = pl.ds(pl.multiple_of(j * COLS, COLS), COLS)
        rows_token = jnp.dot(pick_token, tokens_ref[:, cols], preferred_element_type=jnp.float32)
        rows_scaled = jnp.dot(pick_scaled, cotangent_ref[:, cols], preferred_element_type=jnp.float32)
        send[:, cols] = (rows_token + rows_scaled * gate).astype(jnp.bfloat16)

    pl.semaphore_wait(barrier, len(greet))

    def piece_of(k):
        return send.at[pl.ds(pl.multiple_of(peer(k) * PIECE, PIECE), PIECE)]

    def landing(stream, k):
        return buf.at[0, pl.ds(stream * unit + k * PIECE, PIECE)]

    dispatch = {}
    for stream, where in ((0, d), (1, other_face)):
        for k in range(E):
            if stream or k:
                dispatch[stream, k] = pltpu.make_async_remote_copy(
                    src_ref=piece_of(k),
                    dst_ref=landing(stream, k),
                    send_sem=disp_s.at[stream, k],
                    recv_sem=disp_r.at[stream, k],
                    device_id=(peer(k), where),
                    device_id_type=MESH,
                )
    own_piece = pltpu.make_async_copy(piece_of(0), landing(0, 0), local_sem.at[1])
    own_piece.start()
    for k in range(1, near):
        dispatch[0, k].start()
    give_up = pltpu.make_async_remote_copy(
        src_ref=up_ref,
        dst_ref=wbuf.at[c],
        send_sem=up_s,
        recv_sem=up_r,
        device_id=(e, sibling),
        device_id_type=MESH,
    )

    def lies(stream, way, s, h):
        if s == 0:
            b, at = 0, stream * 2 + h
        elif s == half:
            b, at = half, stream * 2 + h
        elif stream == 0:
            b, at = s, way * 2 + h
        elif s == half - 1:
            b, at = 2 * half - 1, (1 - h) * 2 + way
        else:
            b, at = half + s, way * 2 + h
        return buf.at[b, pl.ds(at * part, part)]

    ring = {}
    for stream in range(2):
        for way, neighbour in ((0, ahead), (1, behind)):
            for s in range(half - stream):
                for h in range(2):
                    if (stream == 0 and s == half - 1 and h != way):
                        continue
                    ring[stream, way, s, h] = pltpu.make_async_remote_copy(
                        src_ref=lies(stream, way, s, h),
                        dst_ref=lies(stream, way, s + 1, h),
                        send_sem=ring_s.at[stream, way, s, h],
                        recv_sem=ring_r.at[stream, way, s, h],
                        device_id=(e, neighbour),
                        device_id_type=MESH,
                    )

    faces = {}
    for i, (way, s, h) in enumerate(((0, half, 0), (1, half, 1))):
        faces[way, s, h] = pltpu.make_async_remote_copy(
            src_ref=lies(0, way, s, h),
            dst_ref=lies(1, way, s, h),
            send_sem=face_s.at[i],
            recv_sem=face_r.at[i],
            device_id=(e, other_face),
            device_id_type=MESH,
        )

    def pass_on(stream, way, s, h):
        if (stream, way, s, h) in ring:
            ring[stream, way, s, h].start()
        if stream == 0 and (way, s, h) in faces:
            faces[way, s, h].start()

    def arrive(stream, s, h):
        for way in range(2):
            if (stream, way, s - 1, h) in ring:
                ring[stream, way, s - 1, h].wait_recv()
                pass_on(stream, way, s, h)

    own_piece.wait()
    for k in range(1, near):
        dispatch[0, k].wait_send()
    for k in range(near, E):
        dispatch[0, k].start()
    for h in range(2):
        for k in range(max(1, h * near), (h + 1) * near):
            dispatch[0, k].wait_recv()
        for way in range(2):
            pass_on(0, way, 0, h)
    give_up.start()
    for k in range(E):
        dispatch[1, k].start()

    own_cols = pl.ds(pl.multiple_of(e * width, width), width)
    state, own_state = [], []
    for k in range(1, E):
        for i, (src, dst) in enumerate(((master_ref, far_master), (one_ref, far_one), (two_ref, far_two))):
            state.append(
                pltpu.make_async_remote_copy(
                    src_ref=src.at[peer(k)],
                    dst_ref=dst.at[:, own_cols],
                    send_sem=state_s.at[i, k],
                    recv_sem=state_r.at[i, k],
                    device_id=(peer(k), d),
                    device_id_type=MESH,
                )
            )
            state[-1].start()
    for i, (src, dst) in enumerate(((master_ref, far_master), (one_ref, far_one), (two_ref, far_two))):
        own_state.append(pltpu.make_async_copy(src.at[e], dst.at[:, own_cols], local_sem.at[2 + i]))
        own_state[-1].start()

    own_up.wait()
    give_up.wait_recv()

    def hidden(b, first, rows):
        @pl.loop(0, CORES)
        def _(h):
            up = jnp.dot(buf[b, first : first + rows], wbuf[h], preferred_element_type=jnp.float32)
            up = up / (1.0 + jnp.exp(-up))
            up = up.reshape(rows // PIECE, PIECE, F)[:, :CAP]
            up = jnp.concatenate([jnp.zeros_like(up), up], axis=1).reshape(rows, F)
            acts[pl.ds(pl.multiple_of(h * F, F), F), :rows] = up.T.astype(jnp.bfloat16)

    def product(b, first, rows, cols):
        return jnp.dot(
            acts[:, :rows], buf[b, first : first + rows, cols], preferred_element_type=jnp.float32
        )

    def compute(b, first=0, rows=2 * unit, fresh=False):
        hidden(b, first, rows)

        @pl.loop(0, steps)
        def _(j):
            cols = pl.ds(pl.multiple_of(j * COLS, COLS), COLS)
            if fresh:
                acc[:, cols] = product(b, first, rows, cols)
            else:
                acc[:, cols] += product(b, first, rows, cols)

    for s in range(1, half):
        for h in range(2):
            arrive(0, s, h)
            if s == half - 1 and h == 0:
                for k in range(E):
                    dispatch[1, k].wait_recv()
                for g in range(2):
                    for way in range(2):
                        pass_on(1, way, 0, g)
        compute(s, fresh=s == 1)
    compute(0)
    for h in range(2):
        arrive(0, half, h)
    for s in range(1, half - 1):
        for h in range(2):
            arrive(1, s, h)
        compute(half + s)
    faces[0, half, 0].wait_recv()
    faces[1, half, 1].wait_recv()
    compute(half)
    last = 2 * half - 1
    arrive(1, half - 1, 1)
    compute(last, 0, unit)
    arrive(1, half - 1, 0)
    hidden(last, unit, unit)

    theirs = pl.ds(pl.multiple_of((1 - c) * F, F), F)
    mine = pl.ds(pl.multiple_of(c * F, F), F)
    tail, outs = [], []
    for j in range(steps):
        cols = pl.ds(j * COLS, COLS)
        acc[:, cols] += product(last, unit, unit, cols)
        give[j] = acc[theirs, cols].astype(jnp.bfloat16)
        tail.append(
            pltpu.make_async_remote_copy(
                src_ref=give.at[j],
                dst_ref=take.at[j],
                send_sem=tail_s.at[j],
                recv_sem=tail_r.at[j],
                device_id=(e, sibling),
                device_id_type=MESH,
            )
        )
        tail[-1].start()
    for copy in state:
        copy.wait()
    for copy in own_state:
        copy.wait()
    for j in range(steps):
        cols = pl.ds(j * COLS, COLS)
        tail[j].wait_recv()
        gradient = acc[mine, cols] + take[j].astype(jnp.float32)
        acc[mine, cols] = adam_update(far_master[:, cols], far_one[:, cols], far_two[:, cols], gradient)
        outs.append(pltpu.make_async_copy(acc.at[mine, cols], out_ref.at[:, cols], out_sem.at[j]))
        outs[-1].start()
    for k, copy in dispatch.items():
        if k[0] or k[1] >= near:
            copy.wait_send()
    for copy in [give_up] + list(ring.values()) + list(faces.values()) + tail:
        copy.wait_send()
    for copy in outs:
        copy.wait()


def body(E, Z, tokens, cotangent, experts, gate_weights, w_up, master, moment_one, moment_two):
    T, D = tokens.shape
    F = w_up.shape[2]
    unit = E * PIECE
    half = Z // 2
    anywhere = pl.BlockSpec(memory_space=pl.ANY)
    fresh = pl.pallas_call(
        functools.partial(kernel, E, Z),
        out_shape=jax.ShapeDtypeStruct((F, D), jnp.float32),
        in_specs=[anywhere] * 8,
        out_specs=anywhere,
        scratch_shapes=[
            pltpu.VMEM((2, T), jnp.int32),
            pltpu.VMEM((2, T), jnp.float32),
            pltpu.VMEM((T, D), jnp.bfloat16),
            pltpu.VMEM((T, D), jnp.bfloat16),
            pltpu.VMEM((unit, D), jnp.bfloat16),
            pltpu.VMEM((Z, 2 * unit, D), jnp.bfloat16),
            pltpu.VMEM((CORES, D, F), jnp.bfloat16),
            pltpu.VMEM((CORES * F, 2 * unit), jnp.bfloat16),
            pltpu.VMEM((CORES * F, D), jnp.float32),
            pltpu.VMEM((D // COLS, F, COLS), jnp.bfloat16),
            pltpu.VMEM((D // COLS, F, COLS), jnp.bfloat16),
            pltpu.VMEM((F, D), jnp.float32),
            pltpu.VMEM((F, D), jnp.bfloat16),
            pltpu.VMEM((F, D), jnp.bfloat16),
            pltpu.SemaphoreType.DMA((2, E)),
            pltpu.SemaphoreType.DMA((2, E)),
            pltpu.SemaphoreType.DMA((2, 2, half, 2)),
            pltpu.SemaphoreType.DMA((2, 2, half, 2)),
            pltpu.SemaphoreType.DMA((4,)),
            pltpu.SemaphoreType.DMA((4,)),
            pltpu.SemaphoreType.DMA((3, E)),
            pltpu.SemaphoreType.DMA((3, E)),
            pltpu.SemaphoreType.DMA,
            pltpu.SemaphoreType.DMA,
            pltpu.SemaphoreType.DMA((D // COLS,)),
            pltpu.SemaphoreType.DMA((D // COLS,)),
            pltpu.SemaphoreType.DMA((9,)),
            pltpu.SemaphoreType.DMA((D // COLS,)),
        ],
        compiler_params=pltpu.CompilerParams(
            collective_id=0, has_side_effects=True, vmem_limit_bytes=60 * 1024 * 1024
        ),
    )(experts.T, gate_weights.T, tokens, cotangent, w_up[0], master, moment_one, moment_two)
    return fresh[None]


def solution(mesh):
    E = mesh.shape["expert"]
    Z = mesh.shape["dp"] // (FACES * CORES)
    placed = (
        P(("expert", "dp"), None),
        P(("expert", "dp"), None),
        P(("expert", "dp"), None),
        P(("expert", "dp"), None),
        P("expert", None, "dp"),
        P(None, "dp", "expert"),
        P(None, "dp", "expert"),
        P(None, "dp", "expert"),
    )
    return jax.shard_map(
        functools.partial(body, E, Z),
        mesh=mesh,
        in_specs=placed,
        out_specs=P("expert", "dp", None),
        check_vma=False,
    )
```

time: 168 us -> 141 us (0.84)
  Pallas kernels: 157 us -> 137 us
  other arithmetic: 5.64 us -> 0 us
    pallas_call x1, Pallas kernels: 157 us -> 137 us  [body(): pl.pallas_call(functools.partial(kernel, E, Z), out_shape=jax.ShapeDtypeS...]
    broadcast_in_dim x1 -> x0, other arithmetic: 5.64 us -> none  [body(): return adam_update(far_master, far_one, far_two, grad)[None]]
    unnamed x10 -> x1, local copies, waits for them, and re-layouts: 4.55 us -> 3.89 us
where the time goes in v2:
time: 141 us
  Pallas kernels  137 us (97%)
  local copies, waits for them, and re-layouts  3.89 us (3%)
    pallas_call x1, Pallas kernels, body(): pl.pallas_call(functools.partial(kernel, E, Z), out_shape=jax.ShapeDtypeS...  137 us
    unnamed x1, local copies, waits for them, and re-layouts  3.89 us

profile of v2, /device:TPU:1, one launch (start us, length us, event | category | flops | bytes accessed | tf_op | source)
XLA Modules:
  0.0 141.3 jit_solution(16915051609113642397)
XLA Ops:
  0.0 137.4 %shard_map.82 = f32[256,3072]{1,0:T(8,128)} custom-call(s32[2,16]{1,0:T(2,128)} %bitcast.6, f32[2,16]{1,0:T(2,128)} %bitcast.7, bf16[16,3072]{1,0:T(8,128)(2,1)} %tokens_in.1, bf16[16,3072]{1,0:T(8,128)(2,1)} %cotangent_in.1, bf16[3072,256]{1,0:T(8,128)(2,1)} %bitcast.5, f32[8,256,384]{2,1,0:T(8,128)} %master_ref.1, bf16[8,256,384]{2,1,0:T(8,128)(2,1)} %one_ref.1, ...), custom_call_target="tpu_custom_call" | custom-call | tf_op jit(solution)/shard_map/pallas_call | solution.py:376
  137.4 3.9 %copy.10 = f32[1,256,3072]{2,1,0:T(8,128)} copy(f32[1,256,3072]{2,1,0:T(8,128)} %bitcast.4) | data formatting | bytes 6291456

commit v3 on v2

--- a/solution.py
+++ b/solution.py
@@ -14,6 +14,7 @@
 NEIGHBOURS = 2
 PIECE = 2 * CAP
 COLS = 512
+SETTLE = 8
 
 beta_one = 0.9
 beta_two = 0.95
@@ -54,6 +55,7 @@
     acc,
     give,
     take,
+    extra,
     far_master,
     far_one,
     far_two,
@@ -69,6 +71,10 @@
     up_r,
     tail_s,
     tail_r,
+    share_s,
+    share_r,
+    early_s,
+    early_r,
     local_sem,
     out_sem,
 ):
@@ -177,6 +183,19 @@
                     device_id=(peer(k), where),
                     device_id_type=MESH,
                 )
+    early = [
+        pltpu.make_async_remote_copy(
+            src_ref=piece_of(0),
+            dst_ref=buf.at[1, pl.ds(way * unit, PIECE)],
+            send_sem=early_s.at[way],
+            recv_sem=early_r.at[way],
+            device_id=(e, neighbour),
+            device_id_type=MESH,
+        )
+        for way, neighbour in ((0, ahead), (1, behind))
+    ]
+    for copy in early:
+        copy.start()
     own_piece = pltpu.make_async_copy(piece_of(0), landing(0, 0), local_sem.at[1])
     own_piece.start()
     for k in range(1, near):
@@ -190,7 +209,7 @@
         device_id_type=MESH,
     )
 
-    def lies(stream, way, s, h):
+    def lies(stream, way, s, h, skip=0):
         if s == 0:
             b, at = 0, stream * 2 + h
         elif s == half:
@@ -201,7 +220,7 @@
             b, at = 2 * half - 1, (1 - h) * 2 + way
         else:
             b, at = half + s, way * 2 + h
-        return buf.at[b, pl.ds(at * part, part)]
+        return buf.at[b, pl.ds(at * part + skip, part - skip)]
 
     ring = {}
     for stream in range(2):
@@ -210,9 +229,10 @@
                 for h in range(2):
                     if (stream == 0 and s == half - 1 and h != way):
                         continue
+                    skip = PIECE if (stream, s, h) == (0, 0, 0) else 0
                     ring[stream, way, s, h] = pltpu.make_async_remote_copy(
-                        src_ref=lies(stream, way, s, h),
-                        dst_ref=lies(stream, way, s + 1, h),
+                        src_ref=lies(stream, way, s, h, skip),
+                        dst_ref=lies(stream, way, s + 1, h, skip),
                         send_sem=ring_s.at[stream, way, s, h],
                         recv_sem=ring_r.at[stream, way, s, h],
                         device_id=(e, neighbour),
@@ -240,6 +260,8 @@
         for way in range(2):
             if (stream, way, s - 1, h) in ring:
                 ring[stream, way, s - 1, h].wait_recv()
+                if (stream, s, h) == (0, 1, 0):
+                    early[way].wait_recv()
                 pass_on(stream, way, s, h)
 
     own_piece.wait()
@@ -278,14 +300,18 @@
     own_up.wait()
     give_up.wait_recv()
 
+    def activation(rows_of, weight):
+        rows = rows_of.shape[0]
+        up = jnp.dot(rows_of, weight, preferred_element_type=jnp.float32)
+        up = up / (1.0 + jnp.exp(-up))
+        up = up.reshape(rows // PIECE, PIECE, F)[:, :CAP]
+        up = jnp.concatenate([jnp.zeros_like(up), up], axis=1).reshape(rows, F)
+        return up.T.astype(jnp.bfloat16)
+
     def hidden(b, first, rows):
         @pl.loop(0, CORES)
         def _(h):
-            up = jnp.dot(buf[b, first : first + rows], wbuf[h], preferred_element_type=jnp.float32)
-            up = up / (1.0 + jnp.exp(-up))
-            up = up.reshape(rows // PIECE, PIECE, F)[:, :CAP]
-            up = jnp.concatenate([jnp.zeros_like(up), up], axis=1).reshape(rows, F)
-            acts[pl.ds(pl.multiple_of(h * F, F), F), :rows] = up.T.astype(jnp.bfloat16)
+            acts[pl.ds(pl.multiple_of(h * F, F), F), :rows] = activation(buf[b, first : first + rows], wbuf[h])
 
     def product(b, first, rows, cols):
         return jnp.dot(
@@ -323,19 +349,12 @@
     faces[0, half, 0].wait_recv()
     faces[1, half, 1].wait_recv()
     compute(half)
-    last = 2 * half - 1
-    arrive(1, half - 1, 1)
-    compute(last, 0, unit)
-    arrive(1, half - 1, 0)
-    hidden(last, unit, unit)
 
     theirs = pl.ds(pl.multiple_of((1 - c) * F, F), F)
     mine = pl.ds(pl.multiple_of(c * F, F), F)
     tail, outs = [], []
     for j in range(steps):
-        cols = pl.ds(j * COLS, COLS)
-        acc[:, cols] += product(last, unit, unit, cols)
-        give[j] = acc[theirs, cols].astype(jnp.bfloat16)
+        give[j] = acc[theirs, pl.ds(j * COLS, COLS)].astype(jnp.bfloat16)
         tail.append(
             pltpu.make_async_remote_copy(
                 src_ref=give.at[j],
@@ -347,23 +366,71 @@
             )
         )
         tail[-1].start()
-    for copy in state:
-        copy.wait()
-    for copy in own_state:
-        copy.wait()
+    last = 2 * half - 1
+    shared = [
+        pltpu.make_async_remote_copy(
+            src_ref=buf.at[last, pl.ds((1 - h) * unit, unit)],
+            dst_ref=extra.at[pl.ds((1 - h) * unit, unit)],
+            send_sem=share_s.at[h],
+            recv_sem=share_r.at[h],
+            device_id=(e, sibling),
+            device_id_type=MESH,
+        )
+        for h in range(2)
+    ]
+
+    def both(h, cols):
+        first = (1 - h) * unit
+        own = jnp.dot(acts[:F, :unit], buf[last, first : first + unit, cols], preferred_element_type=jnp.float32)
+        other = jnp.dot(acts[F:, :unit], extra[first : first + unit, cols], preferred_element_type=jnp.float32)
+        return own + other
+
     for j in range(steps):
-        cols = pl.ds(j * COLS, COLS)
         tail[j].wait_recv()
-        gradient = acc[mine, cols] + take[j].astype(jnp.float32)
-        acc[mine, cols] = adam_update(far_master[:, cols], far_one[:, cols], far_two[:, cols], gradient)
-        outs.append(pltpu.make_async_copy(acc.at[mine, cols], out_ref.at[:, cols], out_sem.at[j]))
-        outs[-1].start()
+        acc[mine, pl.ds(j * COLS, COLS)] += take[j].astype(jnp.float32)
+    for h in range(2):
+        first = (1 - h) * unit
+        arrive(1, half - 1, h)
+        shared[h].start()
+        acts[:F, :unit] = activation(buf[last, first : first + unit], wbuf[c])
+        shared[h].wait_recv()
+        acts[F:, :unit] = activation(extra[first : first + unit], wbuf[c])
+        if h == 0:
+            for j in range(steps):
+                cols = pl.ds(j * COLS, COLS)
+                acc[mine, cols] += both(h, cols)
+            for copy in state:
+                copy.wait()
+            for copy in own_state:
+                copy.wait()
+        else:
+            for j in range(steps):
+                cols = pl.ds(j * COLS, COLS)
+                gradient = acc[mine, cols] + both(h, cols)
+                acc[mine, cols] = adam_update(far_master[:, cols], far_one[:, cols], far_two[:, cols], gradient)
+                outs.append(pltpu.make_async_copy(acc.at[mine, cols], out_ref.at[:, cols], out_sem.at[j]))
+                outs[-1].start()
     for k, copy in dispatch.items():
         if k[0] or k[1] >= near:
             copy.wait_send()
-    for copy in [give_up] + list(ring.values()) + list(faces.values()) + tail:
+    for copy in [give_up] + list(ring.values()) + list(faces.values()) + tail + shared + early:
         copy.wait_send()
     for copy in outs:
+        copy.wait()
+
+
+def settle(pieces, src_ref, dst_ref, held, in_sems, out_sems):
+    rows = src_ref.shape[0] // pieces
+    coming, going = [], []
+    for i in range(pieces):
+        at = pl.ds(i * rows, rows)
+        coming.append(pltpu.make_async_copy(src_ref.at[at], held.at[at], in_sems.at[i]))
+        going.append(pltpu.make_async_copy(held.at[at], dst_ref.at[at], out_sems.at[i]))
+        coming[-1].start()
+    for i in range(pieces):
+        coming[i].wait()
+        going[i].start()
+    for copy in going:
         copy.wait()
 
 
@@ -390,6 +457,7 @@
             pltpu.VMEM((CORES * F, D), jnp.float32),
             pltpu.VMEM((D // COLS, F, COLS), jnp.bfloat16),
             pltpu.VMEM((D // COLS, F, COLS), jnp.bfloat16),
+            pltpu.VMEM((2 * unit, D), jnp.bfloat16),
             pltpu.VMEM((F, D), jnp.float32),
             pltpu.VMEM((F, D), jnp.bfloat16),
             pltpu.VMEM((F, D), jnp.bfloat16),
@@ -405,6 +473,10 @@
             pltpu.SemaphoreType.DMA,
             pltpu.SemaphoreType.DMA((D // COLS,)),
             pltpu.SemaphoreType.DMA((D // COLS,)),
+            pltpu.SemaphoreType.DMA((2,)),
+            pltpu.SemaphoreType.DMA((2,)),
+            pltpu.SemaphoreType.DMA((2,)),
+            pltpu.SemaphoreType.DMA((2,)),
             pltpu.SemaphoreType.DMA((9,)),
             pltpu.SemaphoreType.DMA((D // COLS,)),
         ],
@@ -412,7 +484,18 @@
             collective_id=0, has_side_effects=True, vmem_limit_bytes=60 * 1024 * 1024
         ),
     )(experts.T, gate_weights.T, tokens, cotangent, w_up[0], master, moment_one, moment_two)
-    return fresh[None]
+    return pl.pallas_call(
+        functools.partial(settle, SETTLE),
+        out_shape=jax.ShapeDtypeStruct((F, D), jnp.float32),
+        in_specs=[anywhere],
+        out_specs=anywhere,
+        scratch_shapes=[
+            pltpu.VMEM((F, D), jnp.float32),
+            pltpu.SemaphoreType.DMA((SETTLE,)),
+            pltpu.SemaphoreType.DMA((SETTLE,)),
+        ],
+        compiler_params=pltpu.CompilerParams(vmem_limit_bytes=60 * 1024 * 1024),
+    )(fresh)[None]
 
 
 def solution(mesh):

time: 141 us -> 137 us (0.972)
  local copies, waits for them, and re-layouts: 3.89 us -> 0 us
    unnamed x1 -> x0, local copies, waits for them, and re-layouts: 3.89 us -> none
    pallas_call x1, Pallas kernels: 137 us -> 134 us  [body(): pl.pallas_call(functools.partial(kernel, E, Z), out_shape=jax.ShapeDtypeS...]
    pallas_call x0 -> x1, Pallas kernels: none -> 2.79 us  [body(): pl.pallas_call(functools.partial(settle, SETTLE), out_shape=jax.ShapeDtyp...]
where the time goes in v3:
time: 137 us
  Pallas kernels  137 us (100%)
    pallas_call x1, Pallas kernels, body(): pl.pallas_call(functools.partial(kernel, E, Z), out_shape=jax.ShapeDtypeS...  134 us
    pallas_call x1, Pallas kernels, body(): pl.pallas_call(functools.partial(settle, SETTLE), out_shape=jax.ShapeDtyp...  2.79 us

profile of v3, /device:TPU:1, one launch (start us, length us, event | category | flops | bytes accessed | tf_op | source)
XLA Modules:
  0.0 136.8 jit_solution(9336996555570749683)
XLA Ops:
  0.0 134.0 %shard_map.82.src_ref = f32[256,3072]{1,0:T(8,128)} custom-call(s32[2,16]{1,0:T(2,128)} %bitcast.5, f32[2,16]{1,0:T(2,128)} %bitcast.6, bf16[16,3072]{1,0:T(8,128)(2,1)} %tokens_in.1, bf16[16,3072]{1,0:T(8,128)(2,1)} %cotangent_in.1, bf16[3072,256]{1,0:T(8,128)(2,1)} %bitcast.4, f32[8,256,384]{2,1,0:T(8,128)} %master_ref.1, bf16[8,256,384]{2,1,0:T(8,128)(2,1)} %one_ref.1, ...), custom_call_target="tpu_custom_call" | custom-call | tf_op jit(solution)/shard_map/pallas_call | solution.py:443
  134.0 2.8 %shard_map.83 = f32[256,3072]{1,0:T(8,128)} custom-call(f32[256,3072]{1,0:T(8,128)} %shard_map.82.src_ref), custom_call_target="tpu_custom_call" | custom-call | tf_op jit(solution)/shard_map/pallas_call | solution.py:487

commit v4 on v3

--- a/solution.py
+++ b/solution.py
@@ -209,7 +209,7 @@
         device_id_type=MESH,
     )
 
-    def lies(stream, way, s, h, skip=0):
+    def lies(stream, way, s, h, skip=0, rows=None):
         if s == 0:
             b, at = 0, stream * 2 + h
         elif s == half:
@@ -220,7 +220,7 @@
             b, at = 2 * half - 1, (1 - h) * 2 + way
         else:
             b, at = half + s, way * 2 + h
-        return buf.at[b, pl.ds(at * part + skip, part - skip)]
+        return buf.at[b, pl.ds(at * part + skip, rows or part - skip)]
 
     ring = {}
     for stream in range(2):
@@ -230,9 +230,10 @@
                     if (stream == 0 and s == half - 1 and h != way):
                         continue
                     skip = PIECE if (stream, s, h) == (0, 0, 0) else 0
+                    rows = part // 2 if (stream, s, h) == (1, half - 2, 1) else None
                     ring[stream, way, s, h] = pltpu.make_async_remote_copy(
-                        src_ref=lies(stream, way, s, h, skip),
-                        dst_ref=lies(stream, way, s + 1, h, skip),
+                        src_ref=lies(stream, way, s, h, skip, rows),
+                        dst_ref=lies(stream, way, s + 1, h, skip, rows),
                         send_sem=ring_s.at[stream, way, s, h],
                         recv_sem=ring_r.at[stream, way, s, h],
                         device_id=(e, neighbour),
@@ -240,10 +241,10 @@
                     )
 
     faces = {}
-    for i, (way, s, h) in enumerate(((0, half, 0), (1, half, 1))):
+    for i, (way, s, h) in enumerate(((0, half - 1, 1), (1, half - 1, 1), (0, half, 0), (1, half, 1))):
         faces[way, s, h] = pltpu.make_async_remote_copy(
-            src_ref=lies(0, way, s, h),
-            dst_ref=lies(1, way, s, h),
+            src_ref=lies(0, way, s, h, 0 if s == half else part // 2),
+            dst_ref=lies(1, way, s, h, 0 if s == half else part // 2),
             send_sem=face_s.at[i],
             recv_sem=face_r.at[i],
             device_id=(e, other_face),
@@ -279,7 +280,7 @@
         dispatch[1, k].start()
 
     own_cols = pl.ds(pl.multiple_of(e * width, width), width)
-    state, own_state = [], []
+    state, own_state, held = [], [], []
     for k in range(1, E):
         for i, (src, dst) in enumerate(((master_ref, far_master), (one_ref, far_one), (two_ref, far_two))):
             state.append(
@@ -292,7 +293,10 @@
                     device_id_type=MESH,
                 )
             )
-            state[-1].start()
+            if i == 2 and offsets[k][1]:
+                held.append(state[-1])
+            else:
+                state[-1].start()
     for i, (src, dst) in enumerate(((master_ref, far_master), (one_ref, far_one), (two_ref, far_two))):
         own_state.append(pltpu.make_async_copy(src.at[e], dst.at[:, own_cols], local_sem.at[2 + i]))
         own_state[-1].start()
@@ -342,13 +346,17 @@
     compute(0)
     for h in range(2):
         arrive(0, half, h)
+    for copy in held:
+        copy.start()
     for s in range(1, half - 1):
         for h in range(2):
             arrive(1, s, h)
         compute(half + s)
+        if s == 1:
+            compute(half, 0, unit)
     faces[0, half, 0].wait_recv()
     faces[1, half, 1].wait_recv()
-    compute(half)
+    compute(half, unit, unit)
 
     theirs = pl.ds(pl.multiple_of((1 - c) * F, F), F)
     mine = pl.ds(pl.multiple_of(c * F, F), F)
@@ -391,6 +399,9 @@
     for h in range(2):
         first = (1 - h) * unit
         arrive(1, half - 1, h)
+        if h:
+            for way in range(2):
+                faces[way, half - 1, 1].wait_recv()
         shared[h].start()
         acts[:F, :unit] = activation(buf[last, first : first + unit], wbuf[c])
         shared[h].wait_recv()

time: 137 us -> 135 us (0.985)
  Pallas kernels: 137 us -> 134 us
    pallas_call x1, Pallas kernels: 134 us -> 131 us  [body(): pl.pallas_call(functools.partial(kernel, E, Z), out_shape=jax.ShapeDtypeS...]
where the time goes in v4:
time: 135 us; the launch traced here: 134 us
  Pallas kernels  134 us (99%)
    pallas_call x1, Pallas kernels, body(): pl.pallas_call(functools.partial(kernel, E, Z), out_shape=jax.ShapeDtypeS...  131 us
    pallas_call x1, Pallas kernels, body(): pl.pallas_call(functools.partial(settle, SETTLE), out_shape=jax.ShapeDtyp...  2.79 us

profile of v4, /device:TPU:1, one launch (start us, length us, event | category | flops | bytes accessed | tf_op | source)
XLA Modules:
  0.0 134.2 jit_solution(12991576173869555854)
XLA Ops:
  0.0 131.4 %shard_map.82.src_ref = f32[256,3072]{1,0:T(8,128)} custom-call(s32[2,16]{1,0:T(2,128)} %bitcast.5, f32[2,16]{1,0:T(2,128)} %bitcast.6, bf16[16,3072]{1,0:T(8,128)(2,1)} %tokens_in.1, bf16[16,3072]{1,0:T(8,128)(2,1)} %cotangent_in.1, bf16[3072,256]{1,0:T(8,128)(2,1)} %bitcast.4, f32[8,256,384]{2,1,0:T(8,128)} %master_ref.1, bf16[8,256,384]{2,1,0:T(8,128)(2,1)} %one_ref.1, ...), custom_call_target="tpu_custom_call" | custom-call | tf_op jit(solution)/shard_map/pallas_call | solution.py:454
  131.4 2.8 %shard_map.83 = f32[256,3072]{1,0:T(8,128)} custom-call(f32[256,3072]{1,0:T(8,128)} %shard_map.82.src_ref), custom_call_target="tpu_custom_call" | custom-call | tf_op jit(solution)/shard_map/pallas_call | solution.py:498

commit v5 on v4

--- a/solution.py
+++ b/solution.py
@@ -344,10 +344,10 @@
                         pass_on(1, way, 0, g)
         compute(s, fresh=s == 1)
     compute(0)
-    for h in range(2):
-        arrive(0, half, h)
+    arrive(0, half, 0)
     for copy in held:
         copy.start()
+    arrive(0, half, 1)
     for s in range(1, half - 1):
         for h in range(2):
             arrive(1, s, h)

time: 135 us -> 145 us (1.074)
  Pallas kernels: 134 us -> 143 us
    pallas_call x1, Pallas kernels: 131 us -> 141 us  [body(): pl.pallas_call(functools.partial(kernel, E, Z), out_shape=jax.ShapeDtypeS...]
where the time goes in v5:
time: 145 us; the launch traced here: 143 us
  Pallas kernels  143 us (99%)
    pallas_call x1, Pallas kernels, body(): pl.pallas_call(functools.partial(kernel, E, Z), out_shape=jax.ShapeDtypeS...  141 us

profile of v5, /device:TPU:1, one launch (start us, length us, event | category | flops | bytes accessed | tf_op | source)
XLA Modules:
  0.0 143.5 jit_solution(4342857828535134673)
XLA Ops:
  0.0 140.7 %shard_map.82.src_ref = f32[256,3072]{1,0:T(8,128)} custom-call(s32[2,16]{1,0:T(2,128)} %bitcast.5, f32[2,16]{1,0:T(2,128)} %bitcast.6, bf16[16,3072]{1,0:T(8,128)(2,1)} %tokens_in.1, bf16[16,3072]{1,0:T(8,128)(2,1)} %cotangent_in.1, bf16[3072,256]{1,0:T(8,128)(2,1)} %bitcast.4, f32[8,256,384]{2,1,0:T(8,128)} %master_ref.1, bf16[8,256,384]{2,1,0:T(8,128)(2,1)} %one_ref.1, ...), custom_call_target="tpu_custom_call" | custom-call | tf_op jit(solution)/shard_map/pallas_call | solution.py:454
  140.7 2.8 %shard_map.83 = f32[256,3072]{1,0:T(8,128)} custom-call(f32[256,3072]{1,0:T(8,128)} %shard_map.82.src_ref), custom_call_target="tpu_custom_call" | custom-call | tf_op jit(solution)/shard_map/pallas_call | solution.py:498
